TPU v7x, 256 devices: a whole 4x4x8 slice. The times are simulated.
256 devices in a mesh: row: 8 (over z), col: 32 (over x, y, core).
Axes of the slice: x: 4, y: 4, z: 8, core: 2. Of those that a mesh axis runs over, the one named last changes fastest.
Arguments:
- activations: bfloat16 [2, 512, 24, 24, 512], P(None, ('row', 'col')), may hold values from -6 to 6
- out_grads: bfloat16 [2, 512, 24, 24, 256], P(None, ('row', 'col')), may hold values from -6 to 6
- errors: bfloat16 [2, 1179648, 256], P(None, ('row', 'col')), may hold values from -10 to 10
- q_start: float32 [2, 256, 8], replicated, may hold values from -6 to 6
Outputs:
- p_factor: float32 [2, 4608, 8], replicated
- q_factor: float32 [2, 256, 8], replicated
- new_errors: bfloat16 [2, 1179648, 256], P(None, ('row', 'col'))
All inputs are finite; a program needn't handle non-finite values.
Results may differ from a plain program's by a relative error of at most 0.001.
Values sent between devices are 32-bit elements; how exact they have to be, the bound alone decides.
A program may use at most 128 MiB of HBM per device.

v0:
```python
import jax
import jax.numpy as jnp
from jax import lax
from jax.sharding import PartitionSpec as P

grad_scale = 0.03125
epsilon = 1e-06


def local_grad(inputs, upstream):
    side_len = inputs.shape[1]
    padded = jnp.pad(inputs, ((0, 0), (1, 1), (1, 1), (0, 0)))
    flat_up = upstream.reshape(-1, upstream.shape[-1])
    blocks = []
    for tap_row in range(3):
        for tap_col in range(3):
            window = padded[
                :, tap_row : tap_row + side_len, tap_col : tap_col + side_len, :
            ].reshape(-1, inputs.shape[-1])
            blocks.append(
                lax.dot_general(
                    window, flat_up, (((0,), (0,)), ((), ())), preferred_element_type=jnp.float32
                )
            )
    return jnp.concatenate(blocks, axis=0) * grad_scale


def orthonormal(factors):
    columns = []
    for index in range(factors.shape[-1]):
        column = factors[..., index]
        for earlier in columns:
            column = column - jnp.sum(earlier * column, axis=-1, keepdims=True) * earlier
        column = column / jnp.sqrt(jnp.sum(column * column, axis=-1, keepdims=True) + epsilon)
        columns.append(column)
    return jnp.stack(columns, axis=-1)


def finish(merged, start_q, devices):
    highest = lax.Precision.HIGHEST
    p_term = jnp.einsum("gkc,gcr->gkr", merged, start_q, precision=highest)
    p_total = lax.psum(lax.psum(p_term, "row"), "col")
    p_hat = orthonormal(p_total / devices)
    q_term = jnp.einsum("gkc,gkr->gcr", merged, p_hat, precision=highest)
    q_total = lax.psum(lax.psum(q_term, "row"), "col")
    q_mean = q_total / devices
    approx = jnp.einsum("gkr,gcr->gkc", p_hat, q_mean, precision=highest)
    return (p_hat, q_mean, (merged - approx).astype(jnp.bfloat16))


def body(activations, out_grads, errors, q_start):
    devices = lax.axis_size("row") * lax.axis_size("col")
    layers = activations.shape[0]
    p_list = []
    q_list = []
    e_list = []
    for layer_idx in range(layers):
        merged = local_grad(activations[layer_idx], out_grads[layer_idx]) + errors[
            layer_idx
        ].astype(jnp.float32)
        p_one, q_one, e_one = finish(merged[None], q_start[layer_idx : layer_idx + 1], devices)
        p_list.append(p_one)
        q_list.append(q_one)
        e_list.append(e_one)
    p_all = jnp.concatenate(p_list, axis=0)
    q_all = jnp.concatenate(q_list, axis=0)
    e_all = jnp.concatenate(e_list, axis=0)
    return (p_all, q_all, e_all)


def solution(mesh):
    placed = (
        P(None, ("row", "col"), None, None, None),
        P(None, ("row", "col"), None, None, None),
        P(None, ("row", "col"), None),
        P(),
    )
    return jax.shard_map(
        body,
        mesh=mesh,
        in_specs=placed,
        out_specs=(P(), P(), P(None, ("row", "col"), None)),
        check_vma=False,
    )
```

profile of v0, /device:TPU:1, one launch (start us, length us, event | category | flops | bytes accessed | tf_op | source)
XLA Modules:
  0.0 543.2 jit_solution(4503466896199150819)
XLA Ops:
  10.3 7.0 %pad_slice_fusion = (bf16[2,24,24,512]{3,2,1,0:T(8,128)(2,1)S(1)}, bf16[2,24,24,512]{3,2,1,0:T(8,128)(2,1)S(1)}, bf16[2,24,24,512]{3,2,1,0:T(8,128)(2,1)S(1)}, b...) fusion(bf16[2,24,24,512]{3,2,1,0:T(8,128)(2,1)S(1)} %get-tuple-, ...), kind=kLoop, calls=%fused_computation.23 | loop fusion | bytes 21233664 | tf_op jit(solution)/shard_map/slice | solution.py:17
  37.0 5.3 convolution_bitcast_fusion
  42.3 5.1 convolution_bitcast_fusion.1
  65.5 54.1 %all-reduce.11.cloned.1.call-done = (f32[1,4608,8]{1,2,0:T(8,128)}, f32[1,4608,8]{1,2,0:T(8,128)}) async-done(((f32[1,4608,8]{1,2,0:T(8,128)}, f32[1,4608,8]{1,2,0:T(8,128)}), (f32[1,4608,8]{1,2,0:T(8,128)}, f32[1,4608,8]{1,2,0:T(8,128)})) %all-reduce.11.cloned.1.call-update) | async-done | bytes 294928 | tf_op jit(solution)/shard_map/psum | solution.py:42
  121.4 115.7 %all-reduce.9.cloned.1.call-done = (f32[1,4608,8]{1,2,0:T(8,128)}, f32[1,4608,8]{1,2,0:T(8,128)}) async-done(((f32[1,4608,8]{1,2,0:T(8,128)}, f32[1,4608,8]{1,2,0:T(8,128)}), (f32[1,4608,8]{1,2,0:T(8,128)}, f32[1,4608,8]{1,2,0:T(8,128)})) %all-reduce.9.cloned.1.call-update) | async-done | bytes 294928 | tf_op jit(solution)/shard_map/psum | solution.py:42
  243.4 4.6 multiply_reduce_fusion.6
  248.7 4.6 multiply_reduce_fusion.5
  258.1 5.4 %multiply_reduce_fusion.4 = (f32[]{:T(128)}, f32[]{:T(128)}, f32[]{:T(128)}, f32[]{:T(128)}, f32[1,4608]{1,0:T(1,128)S(1)}, /*index=5*/f32[1,4608]{1,0:T(1,128)S(1)}, f32[1,4608]{1,0:T(1,128)S(1)}) fusion(f32[1,4608]{1,0:T(1,128)S(1)} %get-tuple-element.122, f32[1,4608]{1,0:T(1,128)S(1)} %get-tuple-element.121, f32[]{:T(128)} %get-tuple-element.120, ...), kind=kLoop, calls=%fused_computation.158 | loop fusion | flops 101372 | bytes 184364 | tf_op jit(solution)/shard_map/reduce_sum | solution.py:33
  264.2 3.2 multiply_reduce_fusion.3
  272.0 2.6 multiply_reduce_fusion.2
  280.1 18.2 %subtract_divide_fusion = (f32[1,4608,1]{1,2,0:T(1,128)S(1)}, f32[1,4608,1]{1,2,0:T(1,128)S(1)}, f32[1,4608,1]{1,2,0:T(1,128)S(1)}, f32[1,4608,1]{1,2,0:T(1,128)...) fusion(f32[1,4608,1]{1,2,0:T(1,128)S(1)} %get-tuple-element.136, ...), kind=kLoop, calls=%fused_computation.151 | loop fusion | flops 290304 | bytes 276620 | tf_op jit(solution)/shard_map/div | solution.py:34
  298.5 5.8 %fusion.25 = f32[1,256,8]{1,2,0:T(8,128)S(1)} fusion(f32[1,4608,256]{2,1,0:T(8,128)} %copy-done, bf16[2,4608,256]{2,1,0:T(8,128)(2,1)} %param.6, f32[1,4608,8]{1,2,0:T(8,128)S(1)} %stack.5), kind=kOutput, calls=%fused_computation.46 | convolution fusion | flops 116785152 | bytes 7233536 | tf_op jit(solution)/shard_map/gkc,gkr->gcr/dot_general | solution.py:44
  309.8 4.6 multiply_reduce_fusion.35
  315.1 4.5 multiply_reduce_fusion.34
  324.1 5.2 multiply_reduce_fusion.33
  330.0 3.4 multiply_reduce_fusion.32
  338.1 2.7 multiply_reduce_fusion.31
  346.2 18.1 %subtract_divide_fusion.7 = (f32[1,4608,1]{1,2,0:T(1,128)S(1)}, f32[1,4608,1]{1,2,0:T(1,128)S(1)}, f32[1,4608,1]{1,2,0:T(1,128)S(1)}, f32[1,4608,1]{1,2,0:T(1,12...) fusion(f32[1,4608,1]{1,2,0:T(1,128)S(1)} %get-tuple-element.100, ...), kind=kLoop, calls=%fused_computation.207 | loop fusion | flops 290304 | bytes 276620 | tf_op jit(solution)/shard_map/div | solution.py:34
  364.5 5.8 %fusion.22 = f32[1,256,8]{1,2,0:T(8,128)S(1)} fusion(f32[1,4608,256]{2,1,0:T(8,128)} %copy-done.1, bf16[2,4608,256]{2,1,0:T(8,128)(2,1)} %param.6, f32[1,4608,8]{1,2,0:T(8,128)S(1)} %stack.4), kind=kOutput, calls=%fused_computation.45 | convolution fusion | flops 116785152 | bytes 7233536 | tf_op jit(solution)/shard_map/gkc,gkr->gcr/dot_general | solution.py:44
  371.1 23.1 %all-reduce.4 = (f32[1,256,8]{1,2,0:T(8,128)S(1)}, f32[1,256,8]{1,2,0:T(8,128)S(1)}) all-reduce(f32[1,256,8]{1,2,0:T(8,128)S(1)} %fusion.25, f32[1,256,8]{1,2,0:T(8,128)S(1)} %fusion.22), channel_id=1, replica_groups=mesh['row'=8,'col'=32] {'row'}, use_global_device_ids=true, to_apply=%region_78.79 | all-reduce | flops 4096 | bytes 32768 | tf_op jit(solution)/shard_map/psum | solution.py:45
  394.1 126.5 %all-reduce.2 = (f32[1,256,8]{1,2,0:T(8,128)S(1)}, f32[1,256,8]{1,2,0:T(8,128)S(1)}) all-reduce(f32[1,256,8]{1,2,0:T(8,128)S(1)} %get-tuple-element.61, f32[1,256,8]{1,2,0:T(8,128)S(1)} %get-tuple-element.62), channel_id=1, replica_groups=mesh['row'=8,'col'=32] {'col'}, use_global_device_ids=true, to_apply=%region_79.80 | all-reduce | flops 4096 | bytes 32768 | tf_op jit(solution)/shard_map/psum | solution.py:45
  520.7 6.4 %fusion.2 = bf16[1,4608,256]{2,1,0:T(8,128)(2,1)S(1)} fusion(f32[4608,256]{1,0:T(8,128)} %constant_dynamic-update-slice_fusion.8, bf16[2,4608,256]{2,1,0:T(8,128)(2,1)} %param.6, f32[1,4608,8]{1,2,0:T(8,128)S(1)} %stack.5, f32[1,256,8]{1,2,0:T(8,128)S(1)} %get-tuple-element.57), kind=kOutput, calls=%fused_computation.4 | convolution fusion | flops 119146496 | bytes 9592832 | tf_op jit(solution)/shard_map/gkr,gcr->gkc/dot_general | solution.py:47
  527.2 6.0 %fusion.3 = bf16[1,4608,256]{2,1,0:T(8,128)(2,1)S(1)} fusion(f32[4608,256]{1,0:T(8,128)} %constant_dynamic-update-slice_fusion, bf16[2,4608,256]{2,1,0:T(8,128)(2,1)S(1)} %bitcast.333, f32[1,4608,8]{1,2,0:T(8,128)S(1)} %stack.4, f32[1,256,8]{1,2,0:T(8,128)S(1)} %get-tuple-element.58), kind=kOutput, calls=%fused_computation.5 | convolution fusion | flops 119146496 | bytes 9592832 | tf_op jit(solution)/shard_map/gkr,gcr->gkc/dot_general | solution.py:47
  533.8 2.6 pad_maximum_fusion
  (108 shorter events, 77.1 us)
Async XLA Ops:
  7.2 112.4 %all-reduce.11.cloned.1.call-start = ((), (), s32[]{:S(2)}) async-start(), calls=%async_computation.1 | async-start | bytes 589824 | tf_op jit(solution)/shard_map/psum | solution.py:42
  18.7 3.3 copy-start.2
  18.7 3.3 copy-start.9
  31.8 5.2 slice-start
  33.1 3.8 copy-start
  34.5 2.5 copy-start.13
  34.5 2.5 slice-start.1
  37.0 5.3 copy-start.1
  47.4 189.7 %all-reduce.9.cloned.1.call-start = ((), (), s32[]{:S(2)}) async-start(), calls=%async_computation | async-start | bytes 589824 | tf_op jit(solution)/shard_map/psum | solution.py:42
  47.5 8.7 %copy-start.11 = (f32[512,256,1,1]{1,0,3,2:T(8,128)S(1)}, f32[512,256,1,1]{1,0,3,2:T(8,128)}, u32[]{:S(2)}) copy-start(f32[512,256,1,1]{1,0,3,2:T(8,128)} %get-tuple-element.166) | copy-start | bytes 1572868
  47.5 9.5 %copy-start.6 = (f32[512,256]{1,0:T(8,128)S(1)}, f32[512,256]{1,0:T(8,128)}, u32[]{:S(2)}) copy-start(f32[512,256]{1,0:T(8,128)} %get-tuple-element.168) | copy-start | bytes 1572868
  47.5 10.3 %copy-start.7 = (f32[512,256]{1,0:T(8,128)S(1)}, f32[512,256]{1,0:T(8,128)}, u32[]{:S(2)}) copy-start(f32[512,256]{1,0:T(8,128)} %get-tuple-element.170) | copy-start | bytes 1572868
  47.5 11.2 %copy-start.8 = (f32[512,256]{1,0:T(8,128)S(1)}, f32[512,256]{1,0:T(8,128)}, u32[]{:S(2)}) copy-start(f32[512,256]{1,0:T(8,128)} %get-tuple-element.172) | copy-start | bytes 1572868
  52.2 9.9 %copy-start.10 = (f32[512,256,1,1]{1,0,3,2:T(8,128)S(1)}, f32[512,256,1,1]{1,0,3,2:T(8,128)}, u32[]{:S(2)}) copy-start(f32[512,256,1,1]{1,0,3,2:T(8,128)} %get-tuple-element.184) | copy-start | bytes 1572868
  54.2 8.8 %copy-start.3 = (f32[512,256]{1,0:T(8,128)S(1)}, f32[512,256]{1,0:T(8,128)}, u32[]{:S(2)}) copy-start(f32[512,256]{1,0:T(8,128)} %get-tuple-element.174) | copy-start | bytes 1572868
  56.2 7.6 %copy-start.4 = (f32[512,256]{1,0:T(8,128)S(1)}, f32[512,256]{1,0:T(8,128)}, u32[]{:S(2)}) copy-start(f32[512,256]{1,0:T(8,128)} %get-tuple-element.186) | copy-start | bytes 1572868
  57.0 7.6 %copy-start.5 = (f32[512,256]{1,0:T(8,128)S(1)}, f32[512,256]{1,0:T(8,128)}, u32[]{:S(2)}) copy-start(f32[512,256]{1,0:T(8,128)} %get-tuple-element.188) | copy-start | bytes 1572868
  240.2 64.2 %copy-start.12 = (f32[1,4608,8]{1,2,0:T(8,128)S(1)}, f32[1,4608,8]{1,2,0:T(8,128)}, u32[]{:S(2)}) copy-start(f32[1,4608,8]{1,2,0:T(8,128)} %get-tuple-element.60) | copy-start | bytes 442372
  364.5 162.7 %slice-start.2 = ((s8[4718592]{0:T(1024)(128)(4,1)}), s8[524288]{0:T(1024)(128)(4,1)S(1)}, s32[]{:S(2)}) async-start(s8[4718592]{0:T(1024)(128)(4,1)} %bitcast.332), calls=%async_computation.4 | async-start | bytes 1048576
  520.7 6.5 %slice-start.3 = ((s8[4718592]{0:T(1024)(128)(4,1)}), s8[4194304]{0:T(1024)(128)(4,1)S(1)}, s32[]{:S(2)}) async-start(s8[4718592]{0:T(1024)(128)(4,1)} %bitcast.332), calls=%async_computation.5 | async-start | bytes 8388608
Sparse Core Ops, SparseCore 0:
  47.5 71.9 all-reduce.10
  123.3 113.7 all-reduce.8
where the time goes:
time: 547 us; the launch traced here: 543 us
  waiting for transfers between devices  170 us (31%)
  blocking collectives  150 us (27%)
  other arithmetic  114 us (21%)
  matrix products  54 us (10%)
  local copies, waits for them, and re-layouts  30.3 us (6%)
  between operations  25.3 us (5%)
    psum x2, waiting for transfers between devices, finish(): p_total = lax.psum(lax.psum(p_term, 'row'), 'col')  170 us
    psum x2, blocking collectives, finish(): q_total = lax.psum(lax.psum(q_term, 'row'), 'col')  150 us
    reduce_sum x20, other arithmetic, orthonormal(): jnp.sum(earlier * column, axis=-1, keepdims=True) * earlier  57.1 us
    div x2, other arithmetic, orthonormal(): column / jnp.sqrt(jnp.sum(column * column, axis=-1, keepdims=True) + epsi...  36.3 us
    dot_general x18, matrix products, local_grad(): lax.dot_general(window, flat_up, (((0,), (0,)), ((), ())), preferred_elem...  19.6 us
    unnamed x52, local copies, waits for them, and re-layouts  18 us
    reduce_sum x10, other arithmetic, orthonormal(): jnp.sum(column * column, axis=-1, keepdims=True) + epsilon  15.7 us
    dot_general x2, matrix products, finish(): approx = jnp.einsum('gkr,gcr->gkc', p_hat, q_mean, precision=highest)  12.4 us
  transfers between devices with their start and end apart: 2, of which 2 were waited for; matrix products, arithmetic and copies ran while one was open for 4% of the time, Pallas kernels for 0%

commit v1 on v0

v1 whole, which is shorter than its diff:
```python
import functools
import jax
import jax.numpy as jnp
from jax import lax
from jax.experimental import pallas as pl
from jax.experimental.pallas import tpu as pltpu
from jax.sharding import PartitionSpec as P

grad_scale = 0.03125
epsilon = 1e-06
f32 = jnp.float32
bf16 = jnp.bfloat16
MESH = pl.DeviceIdType.MESH

LAYERS, SIDE, PIX, CIN, COUT, RANK, KDIM = 2, 24, 1152, 512, 256, 8, 4608
IMG = SIDE * SIDE
TILES = KDIM // 128
NXY, NZ = 16, 8


def halves(v):
    hi = v.astype(bf16).astype(f32)
    return jnp.concatenate([hi, v - hi], axis=0).astype(bf16)


def dot_nt(a, b):
    return lax.dot_general(a, b, (((1,), (1,)), ((), ())), preferred_element_type=f32)


def dot(a, b):
    return jnp.dot(a, b, preferred_element_type=f32)


def place(shape, axis):
    pix = lax.broadcasted_iota(jnp.int32, shape, axis).astype(f32)
    line = jnp.floor((pix + 0.5) * (1.0 / SIDE))
    col = pix - line * SIDE
    row = line - jnp.floor((line + 0.5) * (1.0 / SIDE)) * SIDE
    return col, row


def orthonormal(layers):
    rank = lax.broadcasted_iota(jnp.int32, (1, RANK, 1), 1)
    layers = list(layers)
    scales = [jnp.zeros((1, RANK, 1), f32) for _ in layers]
    for j in range(RANK):
        for k, c in enumerate(layers):
            cj = c[:, j : j + 1, :]
            prod = c[:TILES] * cj[:TILES]
            dots = jnp.sum(jnp.sum(prod, axis=0, keepdims=True), axis=2, keepdims=True)
            square = dots[:, j : j + 1, :] + epsilon
            scales[k] = jnp.where(rank == j, 1.0 / jnp.sqrt(square), scales[k])
            if j < RANK - 1:
                layers[k] = c - jnp.where(rank > j, dots / square, 0.0) * cj
    return [c * scale for c, scale in zip(layers, scales)]


def far_first(offsets, sizes):
    return sorted(offsets, key=lambda d: -sum(min(i, n - i) for i, n in zip(d, sizes)))


NEAR = far_first([(i, j) for i in range(4) for j in range(4) if i or j], (4, 4))
FAR = far_first([(k,) for k in range(1, NZ)], (NZ,))
PIECES = 1
PROWS = KDIM // PIECES
FIRST, AT_RS, AT_Z = 3, 6, 12


def main_kernel(
    x_hbm, g_hbm, e_hbm, q0_hbm,
    merged, amat, ph_out, q_out,
    xv, gv, ev, qv, xt, gpad, mhi, mlo,
    ws, pbuf, prx, psum, rs_rx, zbuf, pown, pfull, pex, ph, rowop,
    mrx, qx, qz, qf,
    load_sem, send_sem, recv_sem, piece_sem, line_sem,
):
    z = lax.axis_index("row")
    col = lax.axis_index("col")
    core = lax.rem(col, 2)
    chip = col // 2
    other = 1 - core
    partner = (z, chip * 2 + other)
    cx, cy = chip // 4, lax.rem(chip, 4)
    chips = [lax.rem(cx + i, 4) * 4 + lax.rem(cy + j, 4) for i, j in NEAR]
    near = [(z, t * 2 + 1) for t in chips]
    near_0 = [(z, t * 2) for t in chips]
    far = [(lax.rem(z + k, NZ), col) for (k,) in FAR]

    def layer_of(k):
        return other + k * (core - other)

    def load(what, k):
        layer = layer_of(k)
        if what == "q":
            return pltpu.make_async_copy(q0_hbm, qv, load_sem.at[0])
        if what == "g":
            return pltpu.make_async_copy(g_hbm.at[layer], gv.at[layer], load_sem.at[1 + k])
        if what == "x":
            return pltpu.make_async_copy(x_hbm.at[layer], xv.at[layer], load_sem.at[3 + k])
        rows = pl.ds(what * PROWS, PROWS)
        return pltpu.make_async_copy(e_hbm.at[layer, rows], ev.at[layer, rows], load_sem.at[5 + 2 * what + k])

    load("q", 0).start()
    for what, k in [("g", 0), ("g", 1)] + [(what, k) for k in range(2) for what in ("x",) + tuple(range(PIECES))]:
        load(what, k).start()

    barrier = pltpu.get_barrier_semaphore()
    for device in [partner] + near:
        pl.semaphore_signal(barrier, inc=1, device_id=device, device_id_type=MESH)

    @pl.when(core == 1)
    def _():
        for device in near_0 + far:
            pl.semaphore_signal(barrier, inc=1, device_id=device, device_id_type=MESH)

    def send(src, dst, k, device, recv=None):
        pltpu.make_async_remote_copy(
            src_ref=src, dst_ref=dst, send_sem=send_sem.at[k], recv_sem=recv_sem.at[k if recv is None else recv],
            device_id=device, device_id_type=MESH,
        ).start()

    def arrived(ref, k):
        pltpu.make_async_copy(ref, ref, recv_sem.at[k]).wait()

    def sent(ref, k):
        pltpu.make_async_copy(ref, ref, send_sem.at[k]).wait()

    xcol, xrow = place((RANK, PIX), 1)

    load("q", 0).wait()

    @pl.loop(0, 2)
    def _(k):
        layer = layer_of(k)
        q = halves(qv[layer])
        load("g", k).wait()
        u = dot_nt(q, gv[layer])
        u = u[:RANK] + u[RANK:]
        parts = []
        for a in range(3):
            for b in range(3):
                shift = SIDE * (a - 1) + (b - 1)
                part = pltpu.roll(u, shift % PIX, 1) if shift else u
                ok = None
                for tap, pos in ((a, xrow), (b, xcol)):
                    if tap != 1:
                        here = pos < SIDE - 1.5 if tap == 0 else pos > 0.5
                        ok = here if ok is None else jnp.logical_and(ok, here)
                parts.append(part if ok is None else jnp.where(ok, part, 0.0))
        ws[k] = halves(jnp.concatenate(parts, axis=0))

    @pl.loop(0, 2)
    def _(k):
        layer = layer_of(k)
        q = halves(qv[layer])
        load("x", k).wait()
        pg = dot(ws[k], xv[layer])
        pg = (pg[: 9 * RANK] + pg[9 * RANK :]) * grad_scale
        for n in range(PIECES):
            load(n, k).wait()
            pe = dot_nt(q, ev[layer, n * PROWS : (n + 1) * PROWS])
            pe = pe[:RANK] + pe[RANK:]
            for i in range(PROWS // 128):
                t = n * (PROWS // 128) + i
                tap, part = divmod(t, 4)
                tile = pe[:, 128 * i : 128 * i + 128] + pg[RANK * tap : RANK * tap + RANK, 128 * part : 128 * part + 128]
                for r in range(4):
                    pbuf[k, r * 4 + t // 9, t % 9] = tile[2 * r : 2 * r + 2]

        @pl.when(k == 0)
        def _():
            pl.semaphore_wait(barrier, 16 + 22 * core)
            send(pbuf.at[0], prx, 0, partner)

    arrived(prx, 0)
    psum[...] = pbuf[1] + prx[...]

    for t, device in zip(chips, near):
        send(psum.at[t], rs_rx.at[core, chip], 1, device, 10 + core)

    @pl.when(core == 0)
    def _():
        send(psum.at[chip], rs_rx.at[0, chip], 1, partner, 10)

    @pl.when(core == 1)
    def _():
        rs_rx[1, chip] = psum[chip]

    gpad[:, :, :SIDE] = jnp.zeros((3, 2, SIDE, COUT), f32)
    gpad[:, :, SIDE + IMG :] = jnp.zeros((3, 2, SIDE, COUT), f32)

    def prepare(layer):
        xt[...] = jnp.transpose(xv[layer])
        gcol, _ = place((PIX, COUT), 0)
        g = gv[layer].astype(f32)
        for b in range(3):
            if b == 1:
                part = g
            elif b == 0:
                part = jnp.where(gcol < SIDE - 1.5, pltpu.roll(g, PIX - 1, 0), 0.0)
            else:
                part = jnp.where(gcol > 0.5, pltpu.roll(g, 1, 0), 0.0)
            for i in range(2):
                gpad[b, i, SIDE : SIDE + IMG] = part[i * IMG : (i + 1) * IMG]

    def give(tap):
        rows = pl.ds(pl.multiple_of(tap * CIN, CIN), CIN)
        pltpu.make_async_remote_copy(
            src_ref=merged.at[other, rows], dst_ref=mrx.at[rows], send_sem=send_sem.at[9],
            recv_sem=piece_sem.at[tap], device_id=partner, device_id_type=MESH,
        ).start()

    @pl.loop(0, 18)
    def _(step):
        k = step // 9
        tap = step - 9 * k
        layer = layer_of(k)

        @pl.when(tap == 0)
        def _():
            prepare(layer)

        b = lax.rem(tap, 3)
        start = pl.multiple_of(2 * SIDE - SIDE * (tap // 3), 8)
        window = jnp.concatenate([gpad[b, i, pl.ds(start, IMG)] for i in range(2)], axis=0).astype(bf16)
        rows = pl.ds(pl.multiple_of(tap * CIN, CIN), CIN)
        total = dot(xt[...], window) * grad_scale + ev[layer, rows].astype(f32)
        merged[layer, rows] = total

        @pl.when(jnp.logical_or(step < FIRST, jnp.logical_and(step >= AT_RS, step < 8)))
        def _():
            give(tap)

        @pl.when(k == 1)
        def _():
            pltpu.make_async_copy(mrx.at[rows], mrx.at[rows], piece_sem.at[tap]).wait()
            both = total + mrx[rows]
            hi = both.astype(bf16)
            mhi[rows] = hi
            mlo[rows] = (both - hi.astype(f32)).astype(bf16)

        @pl.when(jnp.logical_and(step == AT_RS - 1, core == 1))
        def _():
            arrived(rs_rx.at[0], 10)
            arrived(rs_rx.at[1, pl.ds(0, 15)], 11)
            for i in range(LAYERS):
                part = rs_rx[i, 0]
                for n in range(1, NXY):
                    part = part + rs_rx[i, n]
                zbuf[z, i] = part

            for device in far:
                send(zbuf.at[z], zbuf.at[z], 2, device)

        @pl.when(step == AT_RS - 1)
        def _():
            for n in range(FIRST, AT_RS):
                give(n)

        @pl.when(jnp.logical_and(step == AT_Z - 1, core == 1))
        def _():
            arrived(zbuf.at[pl.ds(0, 7)], 2)
            for i in range(LAYERS):
                part = zbuf[0, i]
                for n in range(1, NZ):
                    part = part + zbuf[n, i]
                part = part * (1.0 / 256.0)
                if i == 0:
                    pown[...] = part
                else:
                    pfull[chip] = part

            def spread(src, k, device):
                pltpu.make_async_remote_copy(
                    src_ref=src, dst_ref=pfull.at[chip], send_sem=send_sem.at[k], recv_sem=line_sem.at[cy],
                    device_id=device, device_id_type=MESH,
                ).start()

            for device_0, device in zip(near_0, near):
                spread(pown, 10, device_0)
                spread(pfull.at[chip], 3, device)
            spread(pown, 10, partner)

        @pl.when(step == AT_Z - 1)
        def _():
            give(8)

    def line(n, total):
        y = lax.rem(cy + n + jnp.where(n == 2, 1, 0) - jnp.where(n == 3, 1, 0), 4)
        here = line_sem.at[y]

        mine = jnp.logical_and(n == 0, core == 1)

        @pl.when(mine)
        def _():
            pltpu.make_async_copy(pfull.at[pl.ds(0, 3)], pfull.at[pl.ds(0, 3)], here).wait()

        @pl.when(jnp.logical_not(mine))
        def _():
            pltpu.make_async_copy(pfull.at[pl.ds(0, 4)], pfull.at[pl.ds(0, 4)], here).wait()

        tiles = pl.ds(9 * y, 9)
        for r in range(4):
            pex[tiles, 2 * r : 2 * r + 2, :] = pfull[4 * r + y]
        left = halves(jnp.concatenate([pex[9 * y + i] for i in range(9)], axis=1))
        rows = pl.ds(pl.multiple_of(y * (KDIM // 4), KDIM // 4), KDIM // 4)
        return total + dot(left, mhi[rows]) + dot(left, mlo[rows])

    right = lax.fori_loop(0, 4, line, jnp.zeros((2 * RANK, COUT), f32))
    qx[core, chip] = right[:RANK] + right[RANK:]
    for device in near:
        send(qx.at[core, chip], qx.at[core, chip], 6, device, 12 + core)

    @pl.when(core == 0)
    def _():
        send(qx.at[0, chip], qx.at[0, chip], 6, partner, 12)

    unit = lax.broadcasted_iota(jnp.int32, (1, RANK, 128), 1) == lax.broadcasted_iota(jnp.int32, (1, RANK, 128), 2)
    unit = jnp.where(unit, 1.0, 0.0).astype(f32)
    (done,) = orthonormal([jnp.concatenate([pex[...], unit], axis=0)])
    ph[core] = done[:TILES]
    send(ph.at[core], ph.at[core], 4, partner)
    for s in range(RANK):
        rowop[core, s] = jnp.broadcast_to(done[TILES][:, s : s + 1], (RANK, COUT))
    send(rowop.at[core], rowop.at[core], 5, partner)

    def for_tail(layer):
        for t in range(0, TILES, 4):
            v = jnp.concatenate([ph[layer, t + k] for k in range(4)], axis=1)
            ph_out[layer, :, 128 * t : 128 * t + 512] = v
            hi = v.astype(bf16).astype(f32)
            both = jnp.concatenate([hi, v - hi, hi, jnp.zeros_like(hi)], axis=0)
            amat[layer, 128 * t : 128 * t + 512] = jnp.transpose(both).astype(bf16)

    for_tail(core)
    @pl.when(core == 1)
    def _():
        arrived(qx.at[0], 12)
        arrived(qx.at[1, pl.ds(0, 15)], 13)
        for i in range(LAYERS):
            part = qx[i, 0]
            for n in range(1, NXY):
                part = part + qx[i, n]
            qz[z, i] = part
        for device in far:
            send(qz.at[z], qz.at[z], 7, device)

    arrived(ph.at[0], 4)
    arrived(rowop.at[0], 5)
    for_tail(other)
    sent(pbuf.at[0], 0)
    sent(ph.at[0], 4)
    sent(rowop.at[0], 5)
    sent(merged.at[0], 9)

    @pl.when(core == 0)
    def _():
        sent(psum, 1)
        sent(qx.at[0], 6)
        arrived(qf, 8)

    @pl.when(core == 1)
    def _():
        sent(psum.at[pl.ds(0, 15)], 1)
        sent(zbuf.at[pl.ds(0, 7)], 2)
        sent(pfull.at[pl.ds(0, 15)], 3)
        sent(pfull, 10)
        sent(qx.at[0, pl.ds(0, 15)], 6)
        sent(qz.at[pl.ds(0, 7)], 7)
        arrived(qz.at[pl.ds(0, 7)], 7)
        for i in range(LAYERS):
            part = qz[0, i]
            for n in range(1, NZ):
                part = part + qz[n, i]
            part = part * (1.0 / 256.0)
            right = rowop[i, 0] * part[0:1]
            for s in range(1, RANK):
                right = right + rowop[i, s] * part[s : s + 1]
            qf[i] = right
        send(qf, qf, 8, partner)
        sent(qf, 8)

    q_out[...] = qf[...]


CHUNK = 256


def tail_kernel(merged, amat, ph, q, p_hbm, q_hbm, e_hbm, stage, sem):
    outs = [pltpu.make_async_copy(ph, p_hbm, sem.at[0]), pltpu.make_async_copy(q, q_hbm, sem.at[1])]
    for copy in outs:
        copy.start()
    for layer in range(LAYERS):
        qh = q[layer]
        hi = qh.astype(bf16).astype(f32)
        right = jnp.concatenate([hi, hi, qh - hi, jnp.zeros_like(hi)], axis=0).astype(bf16)
        for c in range(KDIM // CHUNK):
            rows = slice(c * CHUNK, (c + 1) * CHUNK)
            low = dot(amat[layer, rows], right)
            stage[layer, rows] = (merged[layer, rows] - low).astype(bf16)
            copy = pltpu.make_async_copy(stage.at[layer, rows], e_hbm.at[layer, rows], sem.at[2 + layer * (KDIM // CHUNK) + c])
            copy.start()
            outs.append(copy)
    for copy in outs:
        copy.wait()


def body(activations, out_grads, errors, q_start):
    x = activations.reshape(LAYERS, PIX, CIN)
    g = out_grads.reshape(LAYERS, PIX, COUT)
    q0 = jnp.transpose(q_start, (0, 2, 1))
    x, g, errors, q0 = (pltpu.with_memory_space_constraint(a, pltpu.HBM) for a in (x, g, errors, q0))
    hbm = pl.BlockSpec(memory_space=pltpu.HBM)
    vmem = pl.BlockSpec(memory_space=pltpu.VMEM)
    V = pltpu.VMEM
    chunks = (9, 2, 128)
    merged, amat, ph, q = pl.pallas_call(
        main_kernel,
        out_shape=[
            V((LAYERS, KDIM, COUT), f32),
            V((LAYERS, KDIM, 4 * RANK), bf16),
            V((LAYERS, RANK, KDIM), f32),
            V((LAYERS, RANK, COUT), f32),
        ],
        in_specs=[hbm] * 4,
        out_specs=[vmem] * 4,
        scratch_shapes=[
            V((LAYERS, PIX, CIN), bf16),
            V((LAYERS, PIX, COUT), bf16),
            V((LAYERS, KDIM, COUT), bf16),
            V((LAYERS, RANK, COUT), f32),
            V((CIN, PIX), bf16),
            V((3, 2, IMG + 2 * SIDE, COUT), f32),
            V((KDIM, COUT), bf16),
            V((KDIM, COUT), bf16),
            V((2, 2 * 9 * RANK, PIX), bf16),
            V((2, NXY) + chunks, f32),
            V((NXY,) + chunks, f32),
            V((NXY,) + chunks, f32),
            V((LAYERS, NXY) + chunks, f32),
            V((NZ, LAYERS) + chunks, f32),
            V(chunks, f32),
            V((NXY,) + chunks, f32),
            V((TILES, RANK, 128), f32),
            V((LAYERS, TILES, RANK, 128), f32),
            V((LAYERS, RANK, RANK, COUT), f32),
            V((KDIM, COUT), f32),
            V((LAYERS, NXY, RANK, COUT), f32),
            V((NZ, LAYERS, RANK, COUT), f32),
            V((LAYERS, RANK, COUT), f32),
            pltpu.SemaphoreType.DMA((11,)),
            pltpu.SemaphoreType.DMA((11,)),
            pltpu.SemaphoreType.DMA((14,)),
            pltpu.SemaphoreType.DMA((9,)),
            pltpu.SemaphoreType.DMA((4,)),
        ],
        compiler_params=pltpu.CompilerParams(
            collective_id=0, has_side_effects=True, vmem_limit_bytes=32 << 20
        ),
        cost_estimate=pl.CostEstimate(flops=2 * 2 * KDIM * PIX * COUT, bytes_accessed=9 << 20, transcendentals=0),
        name="factors",
    )(x, g, errors, q0)
    p_t, q_t, new_errors = pl.pallas_call(
        tail_kernel,
        out_shape=[
            jax.ShapeDtypeStruct((LAYERS, RANK, KDIM), f32),
            jax.ShapeDtypeStruct((LAYERS, RANK, COUT), f32),
            jax.ShapeDtypeStruct((LAYERS, KDIM, COUT), bf16),
        ],
        in_specs=[vmem] * 4,
        out_specs=[hbm] * 3,
        scratch_shapes=[V((LAYERS, KDIM, COUT), bf16), pltpu.SemaphoreType.DMA((2 + 2 * (KDIM // CHUNK),))],
        compiler_params=pltpu.CompilerParams(vmem_limit_bytes=32 << 20),
        cost_estimate=pl.CostEstimate(flops=2 * 2 * KDIM * 32 * COUT, bytes_accessed=5 << 20, transcendentals=0),
        name="memory_update",
    )(merged, amat, ph, q)
    return jnp.transpose(p_t, (0, 2, 1)), jnp.transpose(q_t, (0, 2, 1)), new_errors


def solution(mesh):
    placed = (
        P(None, ("row", "col"), None, None, None),
        P(None, ("row", "col"), None, None, None),
        P(None, ("row", "col"), None),
        P(),
    )
    return jax.shard_map(
        body,
        mesh=mesh,
        in_specs=placed,
        out_specs=(P(), P(), P(None, ("row", "col"), None)),
        check_vma=False,
    )
```

time: 547 us -> 41.2 us (0.08)
  waiting for transfers between devices: 170 us -> 0 us
  blocking collectives: 150 us -> 0 us
  other arithmetic: 114 us -> 0 us
  matrix products: 54 us -> 0 us
  Pallas kernels: 0 us -> 40.3 us
  local copies, waits for them, and re-layouts: 30.3 us -> 0 us
  between operations: 25.3 us -> 0.64 us
    psum x2 -> x0, waiting for transfers between devices: 170 us -> none  [finish(): p_total = lax.psum(lax.psum(p_term, 'row'), 'col')]
    psum x2 -> x0, blocking collectives: 150 us -> none  [finish(): q_total = lax.psum(lax.psum(q_term, 'row'), 'col')]
    reduce_sum x30 -> x0, other arithmetic: 72.8 us -> none  [the longest x20 57.1 us: orthonormal(): jnp.sum(earlier * column, axis=-1, keepdims=True) * earlier]
    dot_general x24 -> x0, matrix products: 54 us -> none  [the longest x18 19.6 us: local_grad(): lax.dot_general(window, flat_up, (((0,), (0,)), ((), ())), preferred_elem...]
    pallas_call x0 -> x2, Pallas kernels: none -> 40.3 us  [the longest x1 37.7 us: body(): pl.pallas_call(main_kernel, out_shape=[V((LAYERS, KDIM, COUT), f32), V((L...]
    div x6 -> x0, other arithmetic: 37.3 us -> none  [the longest x2 36.3 us: orthonormal(): column / jnp.sqrt(jnp.sum(column * column, axis=-1, keepdims=True) + epsi...]
    unnamed x52 -> x0, local copies, waits for them, and re-layouts: 18 us -> none
    slice x2 -> x0, local copies, waits for them, and re-layouts: 8.29 us -> none  [the longest x1 6.97 us: local_grad(): padded[:, tap_row:tap_row + side_len, tap_col:tap_col + side_len, :]]
  transfers between devices with their start and end apart: 2 -> 0, of which waited for: 2 -> 0; matrix products, arithmetic and copies ran while one was open for 4% -> 0% of each run, Pallas kernels for 0% -> 0%
where the time goes in v1:
time: 41.2 us; the launch traced here: 41 us
  Pallas kernels  40.3 us (98%)
  between operations  0.64 us (2%)
    pallas_call x1, Pallas kernels, body(): pl.pallas_call(main_kernel, out_shape=[V((LAYERS, KDIM, COUT), f32), V((L...  37.7 us
    pallas_call x1, Pallas kernels, body(): pl.pallas_call(tail_kernel, out_shape=[jax.ShapeDtypeStruct((LAYERS, RANK...  2.68 us

profile of v1, /device:TPU:1, one launch (start us, length us, event | category | flops | bytes accessed | tf_op | source)
XLA Modules:
  0.0 41.0 jit_solution(16534426090093762304)
XLA Ops:
  0.6 37.7 %factors.1 = (f32[2,4608,256]{2,1,0:T(8,128)S(1)}, bf16[2,4608,32]{2,1,0:T(8,128)(2,1)S(1)}, f32[2,8,4608]{2,1,0:T(8,128)S(1)}, f32[2,8,256]{2,1,0:T(8,128)S(1)}) custom-call(bf16[2,1152,512]{2,1,0:T(8,128)(2,1)} %bitcast.5, bf16[2,1152,256]{2,1,0:T(8,128)(2,1)} %bitcast.6, bf16[2,4608,256]{2,1,0:T(8,128)(2,1)} %e_hbm.1, f32[2,8,256]{2,1,0:T(8,128)} %bitcast.8), custom_call_target="tpu_custom_call" | custom-call | flops 5435817984 | bytes 9437184 | tf_op jit(solution)/shard_map/factors/pallas_call | solution.py:417
  38.3 2.7 %memory_update.1 = (f32[2,8,4608]{2,1,0:T(8,128)}, f32[2,8,256]{2,1,0:T(8,128)}, bf16[2,4608,256]{2,1,0:T(8,128)(2,1)}) custom-call(f32[2,4608,256]{2,1,0:T(8,128)S(1)} %get-tuple-element.10.merged, bf16[2,4608,32]{2,1,0:T(8,128)(2,1)S(1)} %get-tuple-element.11.amat, f32[2,8,4608]{2,1,0:T(8,128)S(1)} %get-tuple-element.12.ph, ...), custom_call_target="tpu_custom_call" | custom-call | flops 150994944 | bytes 5242880 | tf_op jit(solution)/shard_map/memory_update/pallas_call | solution.py:463

commit v2 on v1

--- a/solution.py
+++ b/solution.py
@@ -63,7 +63,7 @@
 FAR = far_first([(k,) for k in range(1, NZ)], (NZ,))
 PIECES = 1
 PROWS = KDIM // PIECES
-FIRST, AT_RS, AT_Z = 3, 6, 12
+AT_RS, AT_Z = 2, 4
 
 
 def main_kernel(
@@ -210,34 +210,41 @@
             recv_sem=piece_sem.at[tap], device_id=partner, device_id_type=MESH,
         ).start()
 
-    @pl.loop(0, 18)
+    @pl.loop(0, 6)
     def _(step):
-        k = step // 9
-        tap = step - 9 * k
+        k = step // 3
+        a = step - 3 * k
         layer = layer_of(k)
 
-        @pl.when(tap == 0)
+        @pl.when(a == 0)
         def _():
             prepare(layer)
 
-        b = lax.rem(tap, 3)
-        start = pl.multiple_of(2 * SIDE - SIDE * (tap // 3), 8)
-        window = jnp.concatenate([gpad[b, i, pl.ds(start, IMG)] for i in range(2)], axis=0).astype(bf16)
-        rows = pl.ds(pl.multiple_of(tap * CIN, CIN), CIN)
-        total = dot(xt[...], window) * grad_scale + ev[layer, rows].astype(f32)
-        merged[layer, rows] = total
-
-        @pl.when(jnp.logical_or(step < FIRST, jnp.logical_and(step >= AT_RS, step < 8)))
-        def _():
-            give(tap)
+        start = pl.multiple_of(2 * SIDE - SIDE * a, 8)
+        for b in range(3):
+            window = jnp.concatenate([gpad[b, i, pl.ds(start, IMG)] for i in range(2)], axis=0).astype(bf16)
+            rows = pl.ds(pl.multiple_of((3 * a + b) * CIN, CIN), CIN)
+            merged[layer, rows] = dot(xt[...], window) * grad_scale + ev[layer, rows].astype(f32)
+
+        @pl.when(step == 0)
+        def _():
+            for n in range(3):
+                give(n)
+
+        @pl.when(step == 2)
+        def _():
+            for n in range(6, 8):
+                give(n)
 
         @pl.when(k == 1)
         def _():
-            pltpu.make_async_copy(mrx.at[rows], mrx.at[rows], piece_sem.at[tap]).wait()
-            both = total + mrx[rows]
-            hi = both.astype(bf16)
-            mhi[rows] = hi
-            mlo[rows] = (both - hi.astype(f32)).astype(bf16)
+            for b in range(3):
+                rows = pl.ds(pl.multiple_of((3 * a + b) * CIN, CIN), CIN)
+                pltpu.make_async_copy(mrx.at[rows], mrx.at[rows], piece_sem.at[3 * a + b]).wait()
+                both = merged[layer, rows] + mrx[rows]
+                hi = both.astype(bf16)
+                mhi[rows] = hi
+                mlo[rows] = (both - hi.astype(f32)).astype(bf16)
 
         @pl.when(jnp.logical_and(step == AT_RS - 1, core == 1))
         def _():
@@ -254,7 +261,7 @@
 
         @pl.when(step == AT_RS - 1)
         def _():
-            for n in range(FIRST, AT_RS):
+            for n in range(3, 6):
                 give(n)
 
         @pl.when(jnp.logical_and(step == AT_Z - 1, core == 1))

time: 41.2 us -> 40.1 us (0.973)
  Pallas kernels: 40.3 us -> 39.3 us
    pallas_call x1, Pallas kernels: 37.7 us -> 36.6 us  [body(): pl.pallas_call(main_kernel, out_shape=[V((LAYERS, KDIM, COUT), f32), V((L...]
where the time goes in v2:
time: 40.1 us; the launch traced here: 40 us
  Pallas kernels  39.3 us (98%)
  between operations  0.64 us (2%)
    pallas_call x1, Pallas kernels, body(): pl.pallas_call(main_kernel, out_shape=[V((LAYERS, KDIM, COUT), f32), V((L...  36.6 us
    pallas_call x1, Pallas kernels, body(): pl.pallas_call(tail_kernel, out_shape=[jax.ShapeDtypeStruct((LAYERS, RANK...  2.68 us

profile of v2, /device:TPU:1, one launch (start us, length us, event | category | flops | bytes accessed | tf_op | source)
XLA Modules:
  0.0 40.0 jit_solution(17766384668490391176)
XLA Ops:
  0.6 36.6 %factors.1 = (f32[2,4608,256]{2,1,0:T(8,128)S(1)}, bf16[2,4608,32]{2,1,0:T(8,128)(2,1)S(1)}, f32[2,8,4608]{2,1,0:T(8,128)S(1)}, f32[2,8,256]{2,1,0:T(8,128)S(1)}) custom-call(bf16[2,1152,512]{2,1,0:T(8,128)(2,1)} %bitcast.5, bf16[2,1152,256]{2,1,0:T(8,128)(2,1)} %bitcast.6, bf16[2,4608,256]{2,1,0:T(8,128)(2,1)} %e_hbm.1, f32[2,8,256]{2,1,0:T(8,128)} %bitcast.8), custom_call_target="tpu_custom_call" | custom-call | flops 5435817984 | bytes 9437184 | tf_op jit(solution)/shard_map/factors/pallas_call | solution.py:424
  37.3 2.7 %memory_update.1 = (f32[2,8,4608]{2,1,0:T(8,128)}, f32[2,8,256]{2,1,0:T(8,128)}, bf16[2,4608,256]{2,1,0:T(8,128)(2,1)}) custom-call(f32[2,4608,256]{2,1,0:T(8,128)S(1)} %get-tuple-element.10.merged, bf16[2,4608,32]{2,1,0:T(8,128)(2,1)S(1)} %get-tuple-element.11.amat, f32[2,8,4608]{2,1,0:T(8,128)S(1)} %get-tuple-element.12.ph, ...), custom_call_target="tpu_custom_call" | custom-call | flops 150994944 | bytes 5242880 | tf_op jit(solution)/shard_map/memory_update/pallas_call | solution.py:470

commit v3 on v2

--- a/solution.py
+++ b/solution.py
@@ -71,7 +71,7 @@
     merged, amat, ph_out, q_out,
     xv, gv, ev, qv, xt, gpad, mhi, mlo,
     ws, pbuf, prx, psum, rs_rx, zbuf, pown, pfull, pex, ph, rowop,
-    mrx, qx, qz, qf,
+    mrx, qx, qz,
     load_sem, send_sem, recv_sem, piece_sem, line_sem,
 ):
     z = lax.axis_index("row")
@@ -105,12 +105,12 @@
         load(what, k).start()
 
     barrier = pltpu.get_barrier_semaphore()
-    for device in [partner] + near:
+    for device in [partner] + near + far:
         pl.semaphore_signal(barrier, inc=1, device_id=device, device_id_type=MESH)
 
     @pl.when(core == 1)
     def _():
-        for device in near_0 + far:
+        for device in near_0:
             pl.semaphore_signal(barrier, inc=1, device_id=device, device_id_type=MESH)
 
     def send(src, dst, k, device, recv=None):
@@ -169,7 +169,7 @@
 
         @pl.when(k == 0)
         def _():
-            pl.semaphore_wait(barrier, 16 + 22 * core)
+            pl.semaphore_wait(barrier, 23 + 15 * core)
             send(pbuf.at[0], prx, 0, partner)
 
     arrived(prx, 0)
@@ -351,6 +351,13 @@
             qz[z, i] = part
         for device in far:
             send(qz.at[z], qz.at[z], 7, device)
+        send(qz.at[z], qz.at[z], 8, partner)
+
+    @pl.when(core == 0)
+    def _():
+        arrived(qz.at[0], 8)
+        for device in far:
+            send(qz.at[z], qz.at[z], 7, device)
 
     arrived(ph.at[0], 4)
     arrived(rowop.at[0], 5)
@@ -364,7 +371,6 @@
     def _():
         sent(psum, 1)
         sent(qx.at[0], 6)
-        arrived(qf, 8)
 
     @pl.when(core == 1)
     def _():
@@ -373,21 +379,19 @@
         sent(pfull.at[pl.ds(0, 15)], 3)
         sent(pfull, 10)
         sent(qx.at[0, pl.ds(0, 15)], 6)
-        sent(qz.at[pl.ds(0, 7)], 7)
-        arrived(qz.at[pl.ds(0, 7)], 7)
-        for i in range(LAYERS):
-            part = qz[0, i]
-            for n in range(1, NZ):
-                part = part + qz[n, i]
-            part = part * (1.0 / 256.0)
-            right = rowop[i, 0] * part[0:1]
-            for s in range(1, RANK):
-                right = right + rowop[i, s] * part[s : s + 1]
-            qf[i] = right
-        send(qf, qf, 8, partner)
-        sent(qf, 8)
-
-    q_out[...] = qf[...]
+        sent(qz.at[0], 8)
+
+    sent(qz.at[pl.ds(0, 7)], 7)
+    arrived(qz.at[pl.ds(0, 7)], 7)
+    for i in range(LAYERS):
+        part = qz[0, i]
+        for n in range(1, NZ):
+            part = part + qz[n, i]
+        part = part * (1.0 / 256.0)
+        right = rowop[i, 0] * part[0:1]
+        for s in range(1, RANK):
+            right = right + rowop[i, s] * part[s : s + 1]
+        q_out[i] = right
 
 
 CHUNK = 256
@@ -454,7 +458,6 @@
             V((KDIM, COUT), f32),
             V((LAYERS, NXY, RANK, COUT), f32),
             V((NZ, LAYERS, RANK, COUT), f32),
-            V((LAYERS, RANK, COUT), f32),
             pltpu.SemaphoreType.DMA((11,)),
             pltpu.SemaphoreType.DMA((11,)),
             pltpu.SemaphoreType.DMA((14,)),

time: 40.1 us -> 39.3 us (0.980)
  Pallas kernels: 39.3 us -> 38.5 us
    pallas_call x1, Pallas kernels: 36.6 us -> 35.8 us  [body(): pl.pallas_call(main_kernel, out_shape=[V((LAYERS, KDIM, COUT), f32), V((L...]
where the time goes in v3:
time: 39.3 us; the launch traced here: 39.1 us
  Pallas kernels  38.5 us (98%)
  between operations  0.64 us (2%)
    pallas_call x1, Pallas kernels, body(): pl.pallas_call(main_kernel, out_shape=[V((LAYERS, KDIM, COUT), f32), V((L...  35.8 us
    pallas_call x1, Pallas kernels, body(): pl.pallas_call(tail_kernel, out_shape=[jax.ShapeDtypeStruct((LAYERS, RANK...  2.67 us

profile of v3, /device:TPU:1, one launch (start us, length us, event | category | flops | bytes accessed | tf_op | source)
XLA Modules:
  0.0 39.1 jit_solution(13622371666762568256)
XLA Ops:
  0.6 35.8 %factors.1 = (f32[2,4608,256]{2,1,0:T(8,128)S(1)}, bf16[2,4608,32]{2,1,0:T(8,128)(2,1)S(1)}, f32[2,8,4608]{2,1,0:T(8,128)S(1)}, f32[2,8,256]{2,1,0:T(8,128)S(1)}) custom-call(bf16[2,1152,512]{2,1,0:T(8,128)(2,1)} %bitcast.5, bf16[2,1152,256]{2,1,0:T(8,128)(2,1)} %bitcast.6, bf16[2,4608,256]{2,1,0:T(8,128)(2,1)} %e_hbm.1, f32[2,8,256]{2,1,0:T(8,128)} %bitcast.8), custom_call_target="tpu_custom_call" | custom-call | flops 5435817984 | bytes 9437184 | tf_op jit(solution)/shard_map/factors/pallas_call | solution.py:428
  36.4 2.7 %memory_update.1 = (f32[2,8,4608]{2,1,0:T(8,128)}, f32[2,8,256]{2,1,0:T(8,128)}, bf16[2,4608,256]{2,1,0:T(8,128)(2,1)}) custom-call(f32[2,4608,256]{2,1,0:T(8,128)S(1)} %get-tuple-element.10.merged, bf16[2,4608,32]{2,1,0:T(8,128)(2,1)S(1)} %get-tuple-element.11.amat, f32[2,8,4608]{2,1,0:T(8,128)S(1)} %get-tuple-element.12.ph, ...), custom_call_target="tpu_custom_call" | custom-call | flops 150994944 | bytes 5242880 | tf_op jit(solution)/shard_map/memory_update/pallas_call | solution.py:473

commit v4 on v3

--- a/solution.py
+++ b/solution.py
@@ -190,7 +190,6 @@
     gpad[:, :, SIDE + IMG :] = jnp.zeros((3, 2, SIDE, COUT), f32)
 
     def prepare(layer):
-        xt[...] = jnp.transpose(xv[layer])
         gcol, _ = place((PIX, COUT), 0)
         g = gv[layer].astype(f32)
         for b in range(3):
@@ -216,6 +215,11 @@
         a = step - 3 * k
         layer = layer_of(k)
 
+        @pl.when(step == 0)
+        def _():
+            for i in range(LAYERS):
+                xt[i] = jnp.transpose(xv[i])
+
         @pl.when(a == 0)
         def _():
             prepare(layer)
@@ -224,7 +228,7 @@
         for b in range(3):
             window = jnp.concatenate([gpad[b, i, pl.ds(start, IMG)] for i in range(2)], axis=0).astype(bf16)
             rows = pl.ds(pl.multiple_of((3 * a + b) * CIN, CIN), CIN)
-            merged[layer, rows] = dot(xt[...], window) * grad_scale + ev[layer, rows].astype(f32)
+            merged[layer, rows] = dot(xt[layer], window) * grad_scale + ev[layer, rows].astype(f32)
 
         @pl.when(step == 0)
         def _():
@@ -440,7 +444,7 @@
             V((LAYERS, PIX, COUT), bf16),
             V((LAYERS, KDIM, COUT), bf16),
             V((LAYERS, RANK, COUT), f32),
-            V((CIN, PIX), bf16),
+            V((LAYERS, CIN, PIX), bf16),
             V((3, 2, IMG + 2 * SIDE, COUT), f32),
             V((KDIM, COUT), bf16),
             V((KDIM, COUT), bf16),

time: 39.3 us -> 39.1 us (level)
  no operation moved by 1% of the time
where the time goes in v4:
time: 39.1 us; the launch traced here: 38.9 us
  Pallas kernels  38.2 us (98%)
  between operations  0.64 us (2%)
    pallas_call x1, Pallas kernels, body(): pl.pallas_call(main_kernel, out_shape=[V((LAYERS, KDIM, COUT), f32), V((L...  35.5 us
    pallas_call x1, Pallas kernels, body(): pl.pallas_call(tail_kernel, out_shape=[jax.ShapeDtypeStruct((LAYERS, RANK...  2.68 us

profile of v4, /device:TPU:1, one launch (start us, length us, event | category | flops | bytes accessed | tf_op | source)
XLA Modules:
  0.0 38.9 jit_solution(3775613857971539851)
XLA Ops:
  0.6 35.5 %factors.1 = (f32[2,4608,256]{2,1,0:T(8,128)S(1)}, bf16[2,4608,32]{2,1,0:T(8,128)(2,1)S(1)}, f32[2,8,4608]{2,1,0:T(8,128)S(1)}, f32[2,8,256]{2,1,0:T(8,128)S(1)}) custom-call(bf16[2,1152,512]{2,1,0:T(8,128)(2,1)} %bitcast.5, bf16[2,1152,256]{2,1,0:T(8,128)(2,1)} %bitcast.6, bf16[2,4608,256]{2,1,0:T(8,128)(2,1)} %e_hbm.1, f32[2,8,256]{2,1,0:T(8,128)} %bitcast.8), custom_call_target="tpu_custom_call" | custom-call | flops 5435817984 | bytes 9437184 | tf_op jit(solution)/shard_map/factors/pallas_call | solution.py:432
  36.2 2.7 %memory_update.1 = (f32[2,8,4608]{2,1,0:T(8,128)}, f32[2,8,256]{2,1,0:T(8,128)}, bf16[2,4608,256]{2,1,0:T(8,128)(2,1)}) custom-call(f32[2,4608,256]{2,1,0:T(8,128)S(1)} %get-tuple-element.10.merged, bf16[2,4608,32]{2,1,0:T(8,128)(2,1)S(1)} %get-tuple-element.11.amat, f32[2,8,4608]{2,1,0:T(8,128)S(1)} %get-tuple-element.12.ph, ...), custom_call_target="tpu_custom_call" | custom-call | flops 150994944 | bytes 5242880 | tf_op jit(solution)/shard_map/memory_update/pallas_call | solution.py:477
